TPU v7x, 32 devices: a whole 2x2x4 slice. The times are simulated.
32 devices in a mesh: groups: 2 (over y), seq: 8 (over z, x), ch: 2 (over core).
Axes of the slice: x: 2, y: 2, z: 4, core: 2. Of those that a mesh axis runs over, the one named last changes fastest.
Arguments:
- tokens: int32 [4096], P(('groups', 'seq')), parts along dimension 0, may hold values from 0 to 3
- nuc_table: bfloat16 [3, 4, 4096], P(None, None, 'ch'), may hold values from -6 to 6
- short_filter: float32 [3, 7, 4096], P(None, None, 'ch'), may hold values from -2 to 2
- mr_filter: float32 [256, 128], P('ch'), may hold values from -0.5 to 0.5
- head_weight: bfloat16 [5, 4096, 256], P(None, 'ch'), may hold values from -0.03125 to 0.03125
Outputs:
- annotation: bfloat16 [4096, 256], P(('groups', 'seq')), parts along dimension 0
There are 2 independent parts, one for each index of `groups`. A program takes and returns all parts, laid end to end along the dimension named above; an argument that names none is the same for every part. Nothing has to cross between parts.
Inputs may be any that keep to these rules, and one draw needn't show every extreme that they name: `tokens`: each entry is a nucleotide letter: 0 A, 1 C, 2 G, 3 T; the complement of a is 3 - a. The letters are integers, so they may cross devices packed several to a 16-bit or wider word without losing anything.
All inputs are finite; a program needn't handle non-finite values.
Results may differ from a plain program's by a relative error of at most 0.0049.
Values may be sent and summed in bfloat16 or wider, within the bound.
A program may use at most 128 MiB of HBM per device.

v0:
```python
import functools

import jax
import jax.numpy as jnp
from jax import lax
from jax.experimental import pallas as pl
from jax.experimental.pallas import tpu as pltpu
from jax.sharding import PartitionSpec as P

MESH = pl.DeviceIdType.MESH
CHUNK = 256


def dot(lhs, rhs, lhs_dim=1, rhs_dim=0):
    return lax.dot_general(
        lhs, rhs, (((lhs_dim,), (rhs_dim,)), ((), ())), preferred_element_type=jnp.float32
    )


def kernel(
    seq_count, tok_ref, nuc_ref, short_ref, mr_ref, head_hbm, out_ref,
    head, toeplitz, taps, short8, track, own, left_tok, right_tok, total, other, left_sum, right_sum,
    head_sem, tok_send, tok_recv, sum_send, sum_recv, rim_send, rim_recv,
):
    rows = tok_ref.shape[1]
    filters, span = mr_ref.shape
    channels = nuc_ref.shape[2]
    short_len = short_ref.shape[1]
    head_taps, _, outs = head.shape
    rim = (head_taps - 1) // 2
    width = channels // filters
    letters_count = nuc_ref.shape[1]
    pad = 8
    group = lax.axis_index("groups")
    place = lax.axis_index("seq")
    core = lax.axis_index("ch")
    has_left = place > 0
    has_right = place < seq_count - 1
    left = place - 1
    right = place + 1

    barrier = pltpu.get_barrier_semaphore()
    pl.semaphore_signal(barrier, inc=1, device_id=(group, place, 1 - core), device_id_type=MESH)

    @pl.when(has_left)
    def _():
        for c in range(2):
            pl.semaphore_signal(barrier, inc=1, device_id=(group, left, c), device_id_type=MESH)

    @pl.when(has_right)
    def _():
        for c in range(2):
            pl.semaphore_signal(barrier, inc=1, device_id=(group, right, c), device_id_type=MESH)

    head_copy = pltpu.make_async_copy(head_hbm, head, head_sem)
    head_copy.start()
    own[...] = jnp.broadcast_to(tok_ref[...], own.shape)
    count = 1 + 2 * has_left.astype(jnp.int32) + 2 * has_right.astype(jnp.int32)
    pl.semaphore_wait(barrier, count)

    def tok_copy(side):
        return pltpu.make_async_remote_copy(
            src_ref=own,
            dst_ref=right_tok if side == 0 else left_tok,
            send_sem=tok_send.at[side],
            recv_sem=tok_recv.at[side],
            device_id=(group, left if side == 0 else right, core),
            device_id_type=MESH,
        )

    @pl.when(has_left)
    def _():
        tok_copy(0).start()

    @pl.when(has_right)
    def _():
        tok_copy(1).start()

    for m in range(3):
        short8[0:short_len, :] = short_ref[m]
        short8[short_len:8, :] = jnp.zeros((8 - short_len, channels), jnp.float32)
        taps_f32 = short8[...]
        table = nuc_ref[m].astype(jnp.float32)
        full = jnp.concatenate([taps_f32 * table[n : n + 1] for n in range(letters_count)], axis=0)
        high = full.astype(jnp.bfloat16).astype(jnp.float32)
        both = jnp.concatenate([high, full - high], axis=0)
        taps[m] = both.T.astype(jnp.bfloat16)

    row_id = lax.broadcasted_iota(jnp.int32, (span, span), 0)
    lane_id = lax.broadcasted_iota(jnp.int32, (span, span), 1)

    def build(g, carry):
        wide = jnp.broadcast_to(mr_ref[pl.ds(g, 1), :], (span, span))
        circ = pltpu.roll(wide, 0, 1, stride=1, stride_axis=0)
        before = lane_id < row_id
        toeplitz[g, 0:span] = jnp.where(before, circ, 0.0).astype(jnp.bfloat16)
        toeplitz[g, span : 2 * span] = jnp.where(before, 0.0, circ).astype(jnp.bfloat16)
        return carry

    lax.fori_loop(0, filters, build, 0, unroll=4)

    @pl.when(has_left)
    def _():
        tok_copy(1).wait_recv()

    @pl.when(has_right)
    def _():
        tok_copy(0).wait_recv()

    @pl.when(jnp.logical_not(has_left))
    def _():
        left_tok[...] = jnp.full(left_tok.shape, -1, jnp.int32)

    @pl.when(jnp.logical_not(has_right))
    def _():
        right_tok[...] = jnp.full(right_tok.shape, -1, jnp.int32)

    mid = own[...].astype(jnp.float32)
    ahead = jnp.concatenate([left_tok[...].astype(jnp.float32), mid], axis=1)
    behind = jnp.concatenate([mid, right_tok[...].astype(jnp.float32)], axis=1)
    behind = (letters_count - 1) - behind
    flip = (row_id + lane_id == span - 1).astype(jnp.bfloat16)
    pieces = [
        dot(behind[:, p * span : (p + 1) * span].astype(jnp.bfloat16), flip)
        for p in reversed(range(2 * rows // span))
    ]
    behind = jnp.concatenate(pieces, axis=1)
    hots = []
    for line in (ahead, behind):
        lags = pltpu.roll(line, 0, 1, stride=1, stride_axis=0)[:, rows - span :]
        hot = jnp.concatenate([(lags == n).astype(jnp.float32) for n in range(letters_count)], axis=0)
        hots.append(jnp.concatenate([hot, hot], axis=0).astype(jnp.bfloat16))
    reach = rows + span
    hot_all = jnp.concatenate(hots, axis=1)
    hot_query = jnp.concatenate([h[:, span:] for h in hots], axis=1)
    blocks = rows // span
    perm_row = lax.broadcasted_iota(jnp.int32, (rows, rows), 0)
    perm_lane = lax.broadcasted_iota(jnp.int32, (rows, rows), 1)
    perms = [
        (perm_row == perm_lane).astype(jnp.bfloat16),
        (perm_row + perm_lane == rows - 1).astype(jnp.bfloat16),
    ]
    per_chunk = CHUNK // width

    def work(i, carry):
        at = pl.ds(pl.multiple_of(i * CHUNK, CHUNK), CHUNK)
        key = dot(taps[1, at, :], hot_all)
        value = dot(taps[2, at, :], hot_all)
        query = dot(taps[0, at, :], hot_query)
        gated = (key * value).astype(jnp.bfloat16)
        parts = []
        for g in range(per_chunk):
            lines = slice(g * width, (g + 1) * width)
            stack = jnp.concatenate(
                [
                    gated[lines, s * reach + b * span : s * reach + (b + 2) * span]
                    for s in range(2)
                    for b in range(blocks)
                ],
                axis=0,
            )
            mixed = dot(stack, toeplitz[i * per_chunk + g])
            mixed = jnp.concatenate(
                [mixed[n * width : (n + 1) * width] for n in range(2 * blocks)], axis=1
            )
            parts.append((query[lines] * mixed).astype(jnp.bfloat16))
        chunk_track = jnp.concatenate(parts, axis=0)
        for s in range(2):
            turned = dot(perms[s], chunk_track[:, s * rows : (s + 1) * rows], 1, 1)
            track[s, :, at] = turned.astype(jnp.bfloat16)
        return carry

    lax.fori_loop(0, channels // CHUNK, work, 0)

    head_copy.wait()
    total[...] = jnp.zeros_like(total)
    for d in range(head_taps):
        part = dot(track[0], head[d]) + dot(track[1], head[head_taps - 1 - d])
        begin = pad + rim - d
        total[begin : begin + rows, :] += part

    sum_copy = pltpu.make_async_remote_copy(
        src_ref=total.at[pl.ds(pad, rows)],
        dst_ref=other,
        send_sem=sum_send,
        recv_sem=sum_recv,
        device_id=(group, place, 1 - core),
        device_id_type=MESH,
    )
    sum_copy.start()

    def rim_copy(side, c, from_core):
        begin = 0 if side == 0 else pad + rows
        slots = right_sum if side == 0 else left_sum
        return pltpu.make_async_remote_copy(
            src_ref=total.at[pl.ds(begin, pad)],
            dst_ref=slots.at[from_core],
            send_sem=rim_send.at[side, c],
            recv_sem=rim_recv.at[side, from_core],
            device_id=(group, left if side == 0 else right, c),
            device_id_type=MESH,
        )

    @pl.when(has_left)
    def _():
        for c in range(2):
            rim_copy(0, c, core).start()

    @pl.when(has_right)
    def _():
        for c in range(2):
            rim_copy(1, c, core).start()

    @pl.when(jnp.logical_not(has_left))
    def _():
        left_sum[...] = jnp.zeros_like(left_sum)

    @pl.when(jnp.logical_not(has_right))
    def _():
        right_sum[...] = jnp.zeros_like(right_sum)

    @pl.when(has_left)
    def _():
        tok_copy(0).wait_send()
        for c in range(2):
            rim_copy(0, c, core).wait_send()
            rim_copy(1, 0, c).wait_recv()

    @pl.when(has_right)
    def _():
        tok_copy(1).wait_send()
        for c in range(2):
            rim_copy(1, c, core).wait_send()
            rim_copy(0, 0, c).wait_recv()

    sum_copy.wait()
    zero = jnp.zeros((pad - rim, outs), jnp.float32)
    lead = left_sum[0] + left_sum[1]
    trail = right_sum[0] + right_sum[1]
    line = lax.broadcasted_iota(jnp.int32, (pad, outs), 0)
    lead = jnp.where(line < rim, lead, 0.0)
    trail = jnp.where(line >= pad - rim, trail, 0.0)
    summed = total[pad : pad + rows, :] + other[...]
    del zero
    out_ref[0:16, :] = jnp.concatenate([summed[0:pad] + lead, summed[pad:16]], axis=0).astype(jnp.bfloat16)
    out_ref[16 : rows - 16, :] = summed[16 : rows - 16].astype(jnp.bfloat16)
    out_ref[rows - 16 : rows, :] = jnp.concatenate(
        [summed[rows - 16 : rows - pad], summed[rows - pad :] + trail], axis=0
    ).astype(jnp.bfloat16)


def shards(tokens, nuc_table, short_filter, mr_filter, head_weight):
    rows = tokens.shape[0]
    channels = nuc_table.shape[2]
    filters, span = mr_filter.shape
    outs = head_weight.shape[2]
    seq_count = lax.axis_size("seq")
    vmem = pl.BlockSpec(memory_space=pltpu.VMEM)
    pad = 8
    return pl.pallas_call(
        functools.partial(kernel, seq_count),
        out_shape=jax.ShapeDtypeStruct((rows, outs), jnp.bfloat16),
        in_specs=[vmem] * 4 + [pl.BlockSpec(memory_space=pl.ANY)],
        out_specs=vmem,
        scratch_shapes=[
            pltpu.VMEM(head_weight.shape, jnp.bfloat16),
            pltpu.VMEM((filters, 2 * span, span), jnp.bfloat16),
            pltpu.VMEM((3, channels, 64), jnp.bfloat16),
            pltpu.VMEM((8, channels), jnp.float32),
            pltpu.VMEM((2, rows, channels), jnp.bfloat16),
            pltpu.VMEM((8, rows), jnp.int32),
            pltpu.VMEM((8, rows), jnp.int32),
            pltpu.VMEM((8, rows), jnp.int32),
            pltpu.VMEM((rows + 2 * pad, outs), jnp.float32),
            pltpu.VMEM((rows, outs), jnp.float32),
            pltpu.VMEM((2, pad, outs), jnp.float32),
            pltpu.VMEM((2, pad, outs), jnp.float32),
            pltpu.SemaphoreType.DMA,
            pltpu.SemaphoreType.DMA((2,)),
            pltpu.SemaphoreType.DMA((2,)),
            pltpu.SemaphoreType.DMA,
            pltpu.SemaphoreType.DMA,
            pltpu.SemaphoreType.DMA((2, 2)),
            pltpu.SemaphoreType.DMA((2, 2)),
        ],
        compiler_params=pltpu.CompilerParams(
            collective_id=0, has_side_effects=True, vmem_limit_bytes=48 * 1024 * 1024
        ),
    )(tokens.reshape(1, rows), nuc_table, short_filter, mr_filter, head_weight)


def solution(mesh):
    in_specs = (
        P(("groups", "seq")),
        P(None, None, "ch"),
        P(None, None, "ch"),
        P("ch", None),
        P(None, "ch", None),
    )
    out_specs = P(("groups", "seq"), None)
    return jax.shard_map(shards, mesh=mesh, in_specs=in_specs, out_specs=out_specs, check_vma=False)
```

profile of v0, /device:TPU:0, one launch (start us, length us, event | category | flops | bytes accessed | tf_op | source)
XLA Modules:
  0.0 25.8 jit_solution(3460420460547742536)
XLA Ops:
  0.0 0.0 copy-start
  0.0 2.5 %copy-done = bf16[5,2048,256]{2,1,0:T(8,128)(2,1)S(1)} copy-done((bf16[5,2048,256]{2,1,0:T(8,128)(2,1)S(1)}, bf16[5,2048,256]{2,1,0:T(8,128)(2,1)}, u32[]{:S(2)}) %copy-start) | copy-done | bytes 5242904
  2.5 0.0 copy-start.1
  2.5 0.9 %copy-done.1 = f32[3,7,2048]{2,1,0:T(8,128)S(1)} copy-done((f32[3,7,2048]{2,1,0:T(8,128)S(1)}, f32[3,7,2048]{2,1,0:T(8,128)}, u32[]{:S(2)}) %copy-start.1) | copy-done | bytes 172056
  3.4 0.0 copy-start.2
  3.4 0.8 %copy-done.2 = f32[128,128]{1,0:T(8,128)S(1)} copy-done((f32[128,128]{1,0:T(8,128)S(1)}, f32[128,128]{1,0:T(8,128)}, u32[]{:S(2)}) %copy-start.2) | copy-done | bytes 65560
  4.3 0.0 copy-start.3
  4.3 0.8 %copy-done.3 = bf16[3,4,2048]{2,1,0:T(4,128)(2,1)S(1)} copy-done((bf16[3,4,2048]{2,1,0:T(4,128)(2,1)S(1)}, bf16[3,4,2048]{2,1,0:T(4,128)(2,1)}, u32[]{:S(2)}) %copy-start.3) | copy-done | bytes 49176
  5.1 0.0 copy-start.4
  5.1 0.7 %copy-done.4 = s32[256]{0:T(256)S(1)} copy-done((s32[256]{0:T(256)S(1)}, s32[256]{0:T(256)}, u32[]{:S(2)}) %copy-start.4) | copy-done | bytes 1048
  5.7 19.4 %shard_map.55 = bf16[256,256]{1,0:T(8,128)(2,1)S(1)} custom-call(s32[1,256]{1,0:T(1,128)S(1)} %bitcast.1, bf16[3,4,2048]{2,1,0:T(4,128)(2,1)S(1)} %copy-done.3, f32[3,7,2048]{2,1,0:T(8,128)S(1)} %copy-done.1, f32[128,128]{1,0:T(8,128)S(1)} %copy-done.2, bf16[5,2048,256]{2,1,0:T(8,128)(2,1)S(1)} %copy-done), custom_call_target="tpu_custom_call" | custom-call | tf_op jit(solution)/shard_map/pallas_call | solution.py:260
  25.1 0.7 %copy.7 = bf16[256,256]{1,0:T(8,128)(2,1)} copy(bf16[256,256]{1,0:T(8,128)(2,1)S(1)} %shard_map.55) | data formatting | bytes 262144
Async XLA Ops:
  0.0 2.5 %copy-start = (bf16[5,2048,256]{2,1,0:T(8,128)(2,1)S(1)}, bf16[5,2048,256]{2,1,0:T(8,128)(2,1)}, u32[]{:S(2)}) copy-start(bf16[5,2048,256]{2,1,0:T(8,128)(2,1)} %head_hbm.1) | copy-start | bytes 15728644
  2.5 0.9 %copy-start.1 = (f32[3,7,2048]{2,1,0:T(8,128)S(1)}, f32[3,7,2048]{2,1,0:T(8,128)}, u32[]{:S(2)}) copy-start(f32[3,7,2048]{2,1,0:T(8,128)} %short_ref.1) | copy-start | bytes 516100
  3.4 0.8 %copy-start.2 = (f32[128,128]{1,0:T(8,128)S(1)}, f32[128,128]{1,0:T(8,128)}, u32[]{:S(2)}) copy-start(f32[128,128]{1,0:T(8,128)} %mr_ref.1) | copy-start | bytes 196612
  4.3 0.8 %copy-start.3 = (bf16[3,4,2048]{2,1,0:T(4,128)(2,1)S(1)}, bf16[3,4,2048]{2,1,0:T(4,128)(2,1)}, u32[]{:S(2)}) copy-start(bf16[3,4,2048]{2,1,0:T(4,128)(2,1)} %nuc_ref.1) | copy-start | bytes 147460
  5.1 0.7 %copy-start.4 = (s32[256]{0:T(256)S(1)}, s32[256]{0:T(256)}, u32[]{:S(2)}) copy-start(s32[256]{0:T(256)} %param.5) | copy-start | bytes 3076
where the time goes:
time: 26 us; the launch traced here: 25.8 us
  Pallas kernels  19.4 us (75%)
  local copies, waits for them, and re-layouts  6.39 us (25%)
    pallas_call x1, Pallas kernels, shards(): pl.pallas_call(functools.partial(kernel, seq_count), out_shape=jax.ShapeD...  19.4 us
    unnamed x11, local copies, waits for them, and re-layouts  6.39 us

commit v1 on v0

--- a/solution.py
+++ b/solution.py
@@ -18,9 +18,9 @@
 
 
 def kernel(
-    seq_count, tok_ref, nuc_ref, short_ref, mr_ref, head_hbm, out_ref,
-    head, toeplitz, taps, short8, track, own, left_tok, right_tok, total, other, left_sum, right_sum,
-    head_sem, tok_send, tok_recv, sum_send, sum_recv, rim_send, rim_recv,
+    seq_count, tok_hbm, nuc_hbm, short_hbm, mr_hbm, head_hbm, out_ref,
+    tok_ref, nuc_ref, short_ref, mr_ref, head, toeplitz, taps, short8, track, own, left_tok, right_tok, total, other, left_sum, right_sum,
+    load_sem, tok_send, tok_recv, sum_send, sum_recv, rim_send, rim_recv,
 ):
     rows = tok_ref.shape[1]
     filters, span = mr_ref.shape
@@ -52,9 +52,28 @@
         for c in range(2):
             pl.semaphore_signal(barrier, inc=1, device_id=(group, right, c), device_id_type=MESH)
 
-    head_copy = pltpu.make_async_copy(head_hbm, head, head_sem)
-    head_copy.start()
+    loads = [
+        pltpu.make_async_copy(source, target, load_sem.at[n])
+        for n, (source, target) in enumerate(
+            [(tok_hbm, tok_ref), (short_hbm, short_ref), (nuc_hbm, nuc_ref), (mr_hbm, mr_ref), (head_hbm, head)]
+        )
+    ]
+    for load in loads:
+        load.start()
+    loads[0].wait()
     own[...] = jnp.broadcast_to(tok_ref[...], own.shape)
+    loads[1].wait()
+    loads[2].wait()
+    for m in range(3):
+        short8[0:short_len, :] = short_ref[m]
+        short8[short_len:8, :] = jnp.zeros((8 - short_len, channels), jnp.float32)
+        taps_f32 = short8[...]
+        table = nuc_ref[m].astype(jnp.float32)
+        full = jnp.concatenate([taps_f32 * table[n : n + 1] for n in range(letters_count)], axis=0)
+        high = full.astype(jnp.bfloat16).astype(jnp.float32)
+        both = jnp.concatenate([high, full - high], axis=0)
+        taps[m] = both.T.astype(jnp.bfloat16)
+
     count = 1 + 2 * has_left.astype(jnp.int32) + 2 * has_right.astype(jnp.int32)
     pl.semaphore_wait(barrier, count)
 
@@ -76,25 +95,18 @@
     def _():
         tok_copy(1).start()
 
-    for m in range(3):
-        short8[0:short_len, :] = short_ref[m]
-        short8[short_len:8, :] = jnp.zeros((8 - short_len, channels), jnp.float32)
-        taps_f32 = short8[...]
-        table = nuc_ref[m].astype(jnp.float32)
-        full = jnp.concatenate([taps_f32 * table[n : n + 1] for n in range(letters_count)], axis=0)
-        high = full.astype(jnp.bfloat16).astype(jnp.float32)
-        both = jnp.concatenate([high, full - high], axis=0)
-        taps[m] = both.T.astype(jnp.bfloat16)
-
     row_id = lax.broadcasted_iota(jnp.int32, (span, span), 0)
     lane_id = lax.broadcasted_iota(jnp.int32, (span, span), 1)
 
+    loads[3].wait()
+    before = (lane_id < row_id).astype(jnp.bfloat16)
+
     def build(g, carry):
         wide = jnp.broadcast_to(mr_ref[pl.ds(g, 1), :], (span, span))
-        circ = pltpu.roll(wide, 0, 1, stride=1, stride_axis=0)
-        before = lane_id < row_id
-        toeplitz[g, 0:span] = jnp.where(before, circ, 0.0).astype(jnp.bfloat16)
-        toeplitz[g, span : 2 * span] = jnp.where(before, 0.0, circ).astype(jnp.bfloat16)
+        circ = pltpu.roll(wide, 0, 1, stride=1, stride_axis=0).astype(jnp.bfloat16)
+        upper = circ * before
+        toeplitz[g, 0:span] = upper
+        toeplitz[g, span : 2 * span] = circ - upper
         return carry
 
     lax.fori_loop(0, filters, build, 0, unroll=4)
@@ -170,24 +182,23 @@
             track[s, :, at] = turned.astype(jnp.bfloat16)
         return carry
 
-    lax.fori_loop(0, channels // CHUNK, work, 0)
-
-    head_copy.wait()
+    lax.fori_loop(0, channels // CHUNK, work, 0, unroll=True)
+
+    loads[4].wait()
     total[...] = jnp.zeros_like(total)
-    for d in range(head_taps):
-        part = dot(track[0], head[d]) + dot(track[1], head[head_taps - 1 - d])
-        begin = pad + rim - d
-        total[begin : begin + rows, :] += part
-
-    sum_copy = pltpu.make_async_remote_copy(
-        src_ref=total.at[pl.ds(pad, rows)],
-        dst_ref=other,
-        send_sem=sum_send,
-        recv_sem=sum_recv,
-        device_id=(group, place, 1 - core),
-        device_id_type=MESH,
-    )
-    sum_copy.start()
+    half = rows // 2
+    cut = pad + half - 8
+
+    def sum_copy(part):
+        lines = pl.ds(pad, cut - pad) if part == 0 else pl.ds(cut, rows + pad - cut)
+        return pltpu.make_async_remote_copy(
+            src_ref=total.at[lines],
+            dst_ref=other.at[lines],
+            send_sem=sum_send.at[part],
+            recv_sem=sum_recv.at[part],
+            device_id=(group, place, 1 - core),
+            device_id_type=MESH,
+        )
 
     def rim_copy(side, c, from_core):
         begin = 0 if side == 0 else pad + rows
@@ -201,15 +212,18 @@
             device_id_type=MESH,
         )
 
-    @pl.when(has_left)
-    def _():
-        for c in range(2):
-            rim_copy(0, c, core).start()
-
-    @pl.when(has_right)
-    def _():
-        for c in range(2):
-            rim_copy(1, c, core).start()
+    for part in range(2):
+        for d in range(head_taps):
+            lines = slice(part * half, (part + 1) * half)
+            term = dot(track[0, lines], head[d]) + dot(track[1, lines], head[head_taps - 1 - d])
+            begin = pad + rim - d + part * half
+            total[begin : begin + half, :] += term
+        sum_copy(part).start()
+
+        @pl.when(has_left if part == 0 else has_right)
+        def _():
+            for c in range(2):
+                rim_copy(part, c, core).start()
 
     @pl.when(jnp.logical_not(has_left))
     def _():
@@ -233,15 +247,11 @@
             rim_copy(1, c, core).wait_send()
             rim_copy(0, 0, c).wait_recv()
 
-    sum_copy.wait()
-    zero = jnp.zeros((pad - rim, outs), jnp.float32)
+    sum_copy(0).wait()
+    sum_copy(1).wait()
     lead = left_sum[0] + left_sum[1]
     trail = right_sum[0] + right_sum[1]
-    line = lax.broadcasted_iota(jnp.int32, (pad, outs), 0)
-    lead = jnp.where(line < rim, lead, 0.0)
-    trail = jnp.where(line >= pad - rim, trail, 0.0)
-    summed = total[pad : pad + rows, :] + other[...]
-    del zero
+    summed = total[pad : pad + rows, :] + other[pad : pad + rows, :]
     out_ref[0:16, :] = jnp.concatenate([summed[0:pad] + lead, summed[pad:16]], axis=0).astype(jnp.bfloat16)
     out_ref[16 : rows - 16, :] = summed[16 : rows - 16].astype(jnp.bfloat16)
     out_ref[rows - 16 : rows, :] = jnp.concatenate(
@@ -260,9 +270,13 @@
     return pl.pallas_call(
         functools.partial(kernel, seq_count),
         out_shape=jax.ShapeDtypeStruct((rows, outs), jnp.bfloat16),
-        in_specs=[vmem] * 4 + [pl.BlockSpec(memory_space=pl.ANY)],
+        in_specs=[pl.BlockSpec(memory_space=pltpu.HBM)] * 5,
         out_specs=vmem,
         scratch_shapes=[
+            pltpu.VMEM((1, rows), jnp.int32),
+            pltpu.VMEM(nuc_table.shape, jnp.bfloat16),
+            pltpu.VMEM(short_filter.shape, jnp.float32),
+            pltpu.VMEM(mr_filter.shape, jnp.float32),
             pltpu.VMEM(head_weight.shape, jnp.bfloat16),
             pltpu.VMEM((filters, 2 * span, span), jnp.bfloat16),
             pltpu.VMEM((3, channels, 64), jnp.bfloat16),
@@ -272,19 +286,19 @@
             pltpu.VMEM((8, rows), jnp.int32),
             pltpu.VMEM((8, rows), jnp.int32),
             pltpu.VMEM((rows + 2 * pad, outs), jnp.float32),
-            pltpu.VMEM((rows, outs), jnp.float32),
+            pltpu.VMEM((rows + 2 * pad, outs), jnp.float32),
             pltpu.VMEM((2, pad, outs), jnp.float32),
             pltpu.VMEM((2, pad, outs), jnp.float32),
-            pltpu.SemaphoreType.DMA,
+            pltpu.SemaphoreType.DMA((5,)),
             pltpu.SemaphoreType.DMA((2,)),
             pltpu.SemaphoreType.DMA((2,)),
-            pltpu.SemaphoreType.DMA,
-            pltpu.SemaphoreType.DMA,
+            pltpu.SemaphoreType.DMA((2,)),
+            pltpu.SemaphoreType.DMA((2,)),
             pltpu.SemaphoreType.DMA((2, 2)),
             pltpu.SemaphoreType.DMA((2, 2)),
         ],
         compiler_params=pltpu.CompilerParams(
-            collective_id=0, has_side_effects=True, vmem_limit_bytes=48 * 1024 * 1024
+            collective_id=0, has_side_effects=True, vmem_limit_bytes=63 * 1024 * 1024
         ),
     )(tokens.reshape(1, rows), nuc_table, short_filter, mr_filter, head_weight)
 

time: 26 us -> 19.9 us (0.77)
  the two profiles are of different devices: /device:TPU:0 before, /device:TPU:9 now
where the time goes in v1:
time: 19.9 us; the launch traced here: 19.8 us
  Pallas kernels  18.2 us (91%)
  local copies, waits for them, and re-layouts  1.57 us (8%)
    pallas_call x1, Pallas kernels, shards(): pl.pallas_call(functools.partial(kernel, seq_count), out_shape=jax.ShapeD...  18.2 us
    unnamed x1, local copies, waits for them, and re-layouts  1.57 us

profile of v1, /device:TPU:9, one launch (start us, length us, event | category | flops | bytes accessed | tf_op | source)
XLA Modules:
  0.0 19.8 jit_solution(15149939112768571306)
XLA Ops:
  0.0 18.2 %shard_map.55 = bf16[256,256]{1,0:T(8,128)(2,1)} custom-call(s32[1,256]{1,0:T(1,128)} %bitcast.1, bf16[3,4,2048]{2,1,0:T(4,128)(2,1)} %nuc_hbm.1, f32[3,7,2048]{2,1,0:T(8,128)} %short_hbm.1, f32[128,128]{1,0:T(8,128)} %mr_hbm.1, bf16[5,2048,256]{2,1,0:T(8,128)(2,1)} %head_hbm.1), custom_call_target="tpu_custom_call" | custom-call | tf_op jit(solution)/shard_map/pallas_call | solution.py:270
  18.2 1.6 %copy.7 = bf16[256,256]{1,0:T(8,128)(2,1)} copy(bf16[256,256]{1,0:T(8,128)(2,1)} %shard_map.55) | data formatting | bytes 262144

commit v2 on v1

--- a/solution.py
+++ b/solution.py
@@ -8,7 +8,6 @@
 from jax.sharding import PartitionSpec as P
 
 MESH = pl.DeviceIdType.MESH
-CHUNK = 256
 
 
 def dot(lhs, rhs, lhs_dim=1, rhs_dim=0):
@@ -109,7 +108,7 @@
         toeplitz[g, span : 2 * span] = circ - upper
         return carry
 
-    lax.fori_loop(0, filters, build, 0, unroll=4)
+    lax.fori_loop(0, filters, build, 0, unroll=16)
 
     @pl.when(has_left)
     def _():
@@ -145,6 +144,9 @@
     reach = rows + span
     hot_all = jnp.concatenate(hots, axis=1)
     hot_query = jnp.concatenate([h[:, span:] for h in hots], axis=1)
+    wide = 2 * span
+    hot_tiles = [hot_all[:, t : t + wide] for t in range(0, 2 * reach, wide)]
+    query_tiles = [hot_query[:, t : t + wide] for t in range(0, 2 * rows, wide)]
     blocks = rows // span
     perm_row = lax.broadcasted_iota(jnp.int32, (rows, rows), 0)
     perm_lane = lax.broadcasted_iota(jnp.int32, (rows, rows), 1)
@@ -152,41 +154,64 @@
         (perm_row == perm_lane).astype(jnp.bfloat16),
         (perm_row + perm_lane == rows - 1).astype(jnp.bfloat16),
     ]
-    per_chunk = CHUNK // width
-
-    def work(i, carry):
-        at = pl.ds(pl.multiple_of(i * CHUNK, CHUNK), CHUNK)
-        key = dot(taps[1, at, :], hot_all)
-        value = dot(taps[2, at, :], hot_all)
-        query = dot(taps[0, at, :], hot_query)
-        gated = (key * value).astype(jnp.bfloat16)
+    part_channels = span
+    per_part = part_channels // width
+    half = rows // 2
+
+    def gate(p):
+        at = slice(p * part_channels, (p + 1) * part_channels)
+        cells = []
+        for hot in hot_tiles:
+            gated = (dot(taps[1, at, :], hot) * dot(taps[2, at, :], hot)).astype(jnp.bfloat16)
+            cells += [gated[:, t : t + span] for t in range(0, hot.shape[1], span)]
+        return cells
+
+    def mix(p, cells):
+        at = slice(p * part_channels, (p + 1) * part_channels)
+        query = jnp.concatenate([dot(taps[0, at, :], hot) for hot in query_tiles], axis=1)
         parts = []
-        for g in range(per_chunk):
+        for g in range(per_part):
             lines = slice(g * width, (g + 1) * width)
             stack = jnp.concatenate(
                 [
-                    gated[lines, s * reach + b * span : s * reach + (b + 2) * span]
+                    jnp.concatenate(
+                        [cells[s * (blocks + 1) + b][lines], cells[s * (blocks + 1) + b + 1][lines]], axis=1
+                    )
                     for s in range(2)
                     for b in range(blocks)
                 ],
                 axis=0,
             )
-            mixed = dot(stack, toeplitz[i * per_chunk + g])
+            mixed = dot(stack, toeplitz[p * per_part + g])
             mixed = jnp.concatenate(
                 [mixed[n * width : (n + 1) * width] for n in range(2 * blocks)], axis=1
             )
             parts.append((query[lines] * mixed).astype(jnp.bfloat16))
-        chunk_track = jnp.concatenate(parts, axis=0)
+        return jnp.concatenate(parts, axis=0)
+
+    def turn(begin, tracks):
+        chunk_track = jnp.concatenate(tracks, axis=0)
+        at = slice(begin * part_channels, (begin + len(tracks)) * part_channels)
         for s in range(2):
-            turned = dot(perms[s], chunk_track[:, s * rows : (s + 1) * rows], 1, 1)
-            track[s, :, at] = turned.astype(jnp.bfloat16)
-        return carry
-
-    lax.fori_loop(0, channels // CHUNK, work, 0, unroll=True)
+            turned = dot(perms[s], chunk_track[:, s * rows : (s + 1) * rows], 1, 1).astype(jnp.bfloat16)
+            for h in range(2):
+                track[h, s * half : (s + 1) * half, at] = turned[h * half : (h + 1) * half]
+
+    part_count = channels // part_channels
+    pending = []
+    cells = gate(0)
+    for p in range(part_count):
+        ahead_cells = gate(p + 1) if p + 1 < part_count else None
+        done = mix(p, cells)
+        cells = ahead_cells
+        pending.append(done)
+        if len(pending) == 3:
+            turn(p - 2, pending[:2])
+            pending = pending[2:]
+    turn(part_count - len(pending), pending)
 
     loads[4].wait()
     total[...] = jnp.zeros_like(total)
-    half = rows // 2
     cut = pad + half - 8
 
     def sum_copy(part):
@@ -214,10 +239,11 @@
 
     for part in range(2):
         for d in range(head_taps):
-            lines = slice(part * half, (part + 1) * half)
-            term = dot(track[0, lines], head[d]) + dot(track[1, lines], head[head_taps - 1 - d])
+            term = dot(track[part], head[d])
             begin = pad + rim - d + part * half
-            total[begin : begin + half, :] += term
+            total[begin : begin + half, :] += term[:half]
+            begin = pad + d - rim + part * half
+            total[begin : begin + half, :] += term[half:]
         sum_copy(part).start()
 
         @pl.when(has_left if part == 0 else has_right)
@@ -252,11 +278,9 @@
     lead = left_sum[0] + left_sum[1]
     trail = right_sum[0] + right_sum[1]
     summed = total[pad : pad + rows, :] + other[pad : pad + rows, :]
-    out_ref[0:16, :] = jnp.concatenate([summed[0:pad] + lead, summed[pad:16]], axis=0).astype(jnp.bfloat16)
-    out_ref[16 : rows - 16, :] = summed[16 : rows - 16].astype(jnp.bfloat16)
-    out_ref[rows - 16 : rows, :] = jnp.concatenate(
-        [summed[rows - 16 : rows - pad], summed[rows - pad :] + trail], axis=0
-    ).astype(jnp.bfloat16)
+    out_ref[0:pad, :] = summed[0:pad] + lead
+    out_ref[pad : rows - pad, :] = summed[pad : rows - pad]
+    out_ref[rows - pad : rows, :] = summed[rows - pad : rows] + trail
 
 
 def shards(tokens, nuc_table, short_filter, mr_filter, head_weight):
@@ -269,7 +293,7 @@
     pad = 8
     return pl.pallas_call(
         functools.partial(kernel, seq_count),
-        out_shape=jax.ShapeDtypeStruct((rows, outs), jnp.bfloat16),
+        out_shape=jax.ShapeDtypeStruct((rows, outs), jnp.float32),
         in_specs=[pl.BlockSpec(memory_space=pltpu.HBM)] * 5,
         out_specs=vmem,
         scratch_shapes=[
@@ -300,7 +324,7 @@
         compiler_params=pltpu.CompilerParams(
             collective_id=0, has_side_effects=True, vmem_limit_bytes=63 * 1024 * 1024
         ),
-    )(tokens.reshape(1, rows), nuc_table, short_filter, mr_filter, head_weight)
+    )(tokens.reshape(1, rows), nuc_table, short_filter, mr_filter, head_weight).astype(jnp.bfloat16)
 
 
 def solution(mesh):

time: 19.9 us -> 19.2 us (0.965)
  other arithmetic: 0 us -> 1.62 us
  local copies, waits for them, and re-layouts: 1.57 us -> 0 us
  Pallas kernels: 18.2 us -> 17.4 us
    convert_element_type x0 -> x1, other arithmetic: none -> 1.62 us  [shards(): return pl.pallas_call(functools.partial(kernel, seq_count), out_shape=jax...]
    unnamed x1 -> x0, local copies, waits for them, and re-layouts: 1.57 us -> none
    pallas_call x1, Pallas kernels: 18.2 us -> 17.4 us  [shards(): pl.pallas_call(functools.partial(kernel, seq_count), out_shape=jax.ShapeD...]
where the time goes in v2:
time: 19.2 us; the launch traced here: 19 us
  Pallas kernels  17.4 us (91%)
  other arithmetic  1.62 us (8%)
    pallas_call x1, Pallas kernels, shards(): pl.pallas_call(functools.partial(kernel, seq_count), out_shape=jax.ShapeD...  17.4 us
    convert_element_type x1, other arithmetic, shards(): return pl.pallas_call(functools.partial(kernel, seq_count), out_shape=jax...  1.62 us

profile of v2, /device:TPU:9, one launch (start us, length us, event | category | flops | bytes accessed | tf_op | source)
XLA Modules:
  0.0 19.0 jit_solution(6109867893866950657)
XLA Ops:
  0.0 17.4 %shard_map.55 = f32[256,256]{1,0:T(8,128)} custom-call(s32[1,256]{1,0:T(1,128)} %bitcast.1, bf16[3,4,2048]{2,1,0:T(4,128)(2,1)} %nuc_hbm.1, f32[3,7,2048]{2,1,0:T(8,128)} %short_hbm.1, f32[128,128]{1,0:T(8,128)} %mr_hbm.1, bf16[5,2048,256]{2,1,0:T(8,128)(2,1)} %head_hbm.1), custom_call_target="tpu_custom_call" | custom-call | tf_op jit(solution)/shard_map/pallas_call | solution.py:294
  17.4 1.6 %convert_element_type.3 = bf16[256,256]{1,0:T(8,128)(2,1)} convert(f32[256,256]{1,0:T(8,128)} %shard_map.55) | non-fusion elementwise | flops 65536 | bytes 393216 | tf_op jit(solution)/shard_map/convert_element_type | solution.py:327

commit v3 on v2

--- a/solution.py
+++ b/solution.py
@@ -100,15 +100,25 @@
     loads[3].wait()
     before = (lane_id < row_id).astype(jnp.bfloat16)
 
-    def build(g, carry):
-        wide = jnp.broadcast_to(mr_ref[pl.ds(g, 1), :], (span, span))
-        circ = pltpu.roll(wide, 0, 1, stride=1, stride_axis=0).astype(jnp.bfloat16)
+    part_channels = span
+    part_count = channels // part_channels
+    per_part = part_channels // width
+    early_parts = part_count // 2
+
+    def build(g):
+        base = pltpu.roll(jnp.broadcast_to(mr_ref[pl.ds(g, 1), :], (8, span)), 0, 1, stride=1, stride_axis=0)
+        turns = [base] + [pltpu.roll(base, n, 1) for n in range(8, span, 8)]
+        circ = jnp.concatenate(turns, axis=0).astype(jnp.bfloat16)
         upper = circ * before
         toeplitz[g, 0:span] = upper
         toeplitz[g, span : 2 * span] = circ - upper
+
+    def build_step(p, carry):
+        for g in range(per_part):
+            build(p * per_part + g)
         return carry
 
-    lax.fori_loop(0, filters, build, 0, unroll=16)
+    lax.fori_loop(0, early_parts, build_step, 0)
 
     @pl.when(has_left)
     def _():
@@ -154,8 +164,6 @@
         (perm_row == perm_lane).astype(jnp.bfloat16),
         (perm_row + perm_lane == rows - 1).astype(jnp.bfloat16),
     ]
-    part_channels = span
-    per_part = part_channels // width
     half = rows // 2
 
     def gate(p):
@@ -197,11 +205,13 @@
             for h in range(2):
                 track[h, s * half : (s + 1) * half, at] = turned[h * half : (h + 1) * half]
 
-    part_count = channels // part_channels
     pending = []
     cells = gate(0)
     for p in range(part_count):
         ahead_cells = gate(p + 1) if p + 1 < part_count else None
+        if p + early_parts < part_count:
+            for g in range(per_part):
+                build((p + early_parts) * per_part + g)
         done = mix(p, cells)
         cells = ahead_cells
         pending.append(done)
@@ -278,9 +288,11 @@
     lead = left_sum[0] + left_sum[1]
     trail = right_sum[0] + right_sum[1]
     summed = total[pad : pad + rows, :] + other[pad : pad + rows, :]
-    out_ref[0:pad, :] = summed[0:pad] + lead
-    out_ref[pad : rows - pad, :] = summed[pad : rows - pad]
-    out_ref[rows - pad : rows, :] = summed[rows - pad : rows] + trail
+    out_ref[0:16, :] = jnp.concatenate([summed[0:pad] + lead, summed[pad:16]], axis=0).astype(jnp.bfloat16)
+    out_ref[16 : rows - 16, :] = summed[16 : rows - 16].astype(jnp.bfloat16)
+    out_ref[rows - 16 : rows, :] = jnp.concatenate(
+        [summed[rows - 16 : rows - pad], summed[rows - pad :] + trail], axis=0
+    ).astype(jnp.bfloat16)
 
 
 def shards(tokens, nuc_table, short_filter, mr_filter, head_weight):
@@ -293,7 +305,7 @@
     pad = 8
     return pl.pallas_call(
         functools.partial(kernel, seq_count),
-        out_shape=jax.ShapeDtypeStruct((rows, outs), jnp.float32),
+        out_shape=jax.ShapeDtypeStruct((rows, outs), jnp.bfloat16),
         in_specs=[pl.BlockSpec(memory_space=pltpu.HBM)] * 5,
         out_specs=vmem,
         scratch_shapes=[
@@ -324,7 +336,7 @@
         compiler_params=pltpu.CompilerParams(
             collective_id=0, has_side_effects=True, vmem_limit_bytes=63 * 1024 * 1024
         ),
-    )(tokens.reshape(1, rows), nuc_table, short_filter, mr_filter, head_weight).astype(jnp.bfloat16)
+    )(tokens.reshape(1, rows), nuc_table, short_filter, mr_filter, head_weight)
 
 
 def solution(mesh):

time: 19.2 us -> 19.1 us (level)
  other arithmetic: 1.62 us -> 0 us
  local copies, waits for them, and re-layouts: 0 us -> 1.57 us
    convert_element_type x1 -> x0, other arithmetic: 1.62 us -> none  [shards(): return pl.pallas_call(functools.partial(kernel, seq_count), out_shape=jax...]
    unnamed x0 -> x1, local copies, waits for them, and re-layouts: none -> 1.57 us
where the time goes in v3:
time: 19.1 us; the launch traced here: 18.9 us
  Pallas kernels  17.3 us (91%)
  local copies, waits for them, and re-layouts  1.57 us (8%)
    pallas_call x1, Pallas kernels, shards(): pl.pallas_call(functools.partial(kernel, seq_count), out_shape=jax.ShapeD...  17.3 us
    unnamed x1, local copies, waits for them, and re-layouts  1.57 us

profile of v3, /device:TPU:9, one launch (start us, length us, event | category | flops | bytes accessed | tf_op | source)
XLA Modules:
  0.0 18.9 jit_solution(12789146519709176585)
XLA Ops:
  0.0 17.3 %shard_map.55 = bf16[256,256]{1,0:T(8,128)(2,1)} custom-call(s32[1,256]{1,0:T(1,128)} %bitcast.1, bf16[3,4,2048]{2,1,0:T(4,128)(2,1)} %nuc_hbm.1, f32[3,7,2048]{2,1,0:T(8,128)} %short_hbm.1, f32[128,128]{1,0:T(8,128)} %mr_hbm.1, bf16[5,2048,256]{2,1,0:T(8,128)(2,1)} %head_hbm.1), custom_call_target="tpu_custom_call" | custom-call | tf_op jit(solution)/shard_map/pallas_call | solution.py:306
  17.3 1.6 %copy.7 = bf16[256,256]{1,0:T(8,128)(2,1)} copy(bf16[256,256]{1,0:T(8,128)(2,1)} %shard_map.55) | data formatting | bytes 262144

commit v4 on v3

--- a/solution.py
+++ b/solution.py
@@ -61,18 +61,6 @@
         load.start()
     loads[0].wait()
     own[...] = jnp.broadcast_to(tok_ref[...], own.shape)
-    loads[1].wait()
-    loads[2].wait()
-    for m in range(3):
-        short8[0:short_len, :] = short_ref[m]
-        short8[short_len:8, :] = jnp.zeros((8 - short_len, channels), jnp.float32)
-        taps_f32 = short8[...]
-        table = nuc_ref[m].astype(jnp.float32)
-        full = jnp.concatenate([taps_f32 * table[n : n + 1] for n in range(letters_count)], axis=0)
-        high = full.astype(jnp.bfloat16).astype(jnp.float32)
-        both = jnp.concatenate([high, full - high], axis=0)
-        taps[m] = both.T.astype(jnp.bfloat16)
-
     count = 1 + 2 * has_left.astype(jnp.int32) + 2 * has_right.astype(jnp.int32)
     pl.semaphore_wait(barrier, count)
 
@@ -97,13 +85,30 @@
     row_id = lax.broadcasted_iota(jnp.int32, (span, span), 0)
     lane_id = lax.broadcasted_iota(jnp.int32, (span, span), 1)
 
+    loads[1].wait()
+    loads[2].wait()
+    for m in range(3):
+        short8[m, 0:short_len, :] = short_ref[m]
+        short8[m, short_len:8, :] = jnp.zeros((8 - short_len, channels), jnp.float32)
+
+    def prepare(begin, end):
+        at = slice(begin, end)
+        for m in range(3):
+            taps_f32 = short8[m, :, at]
+            table = nuc_ref[m, :, at].astype(jnp.float32)
+            full = jnp.concatenate([taps_f32 * table[n : n + 1] for n in range(letters_count)], axis=0)
+            high = full.astype(jnp.bfloat16).astype(jnp.float32)
+            both = jnp.concatenate([high, full - high], axis=0)
+            taps[m, at, :] = both.T.astype(jnp.bfloat16)
+
     loads[3].wait()
     before = (lane_id < row_id).astype(jnp.bfloat16)
 
     part_channels = span
     part_count = channels // part_channels
     per_part = part_channels // width
-    early_parts = part_count // 2
+    early_parts = part_count // 4
+    prepare(0, early_parts * part_channels)
 
     def build(g):
         base = pltpu.roll(jnp.broadcast_to(mr_ref[pl.ds(g, 1), :], (8, span)), 0, 1, stride=1, stride_axis=0)
@@ -210,6 +215,7 @@
     for p in range(part_count):
         ahead_cells = gate(p + 1) if p + 1 < part_count else None
         if p + early_parts < part_count:
+            prepare((p + early_parts) * part_channels, (p + early_parts + 1) * part_channels)
             for g in range(per_part):
                 build((p + early_parts) * per_part + g)
         done = mix(p, cells)
@@ -316,7 +322,7 @@
             pltpu.VMEM(head_weight.shape, jnp.bfloat16),
             pltpu.VMEM((filters, 2 * span, span), jnp.bfloat16),
             pltpu.VMEM((3, channels, 64), jnp.bfloat16),
-            pltpu.VMEM((8, channels), jnp.float32),
+            pltpu.VMEM((3, 8, channels), jnp.float32),
             pltpu.VMEM((2, rows, channels), jnp.bfloat16),
             pltpu.VMEM((8, rows), jnp.int32),
             pltpu.VMEM((8, rows), jnp.int32),

time: 19.1 us -> 19.1 us (level)
  no operation moved by 1% of the time
where the time goes in v4:
time: 19.1 us; the launch traced here: 18.9 us
  Pallas kernels  17.4 us (91%)
  local copies, waits for them, and re-layouts  1.57 us (8%)
    pallas_call x1, Pallas kernels, shards(): pl.pallas_call(functools.partial(kernel, seq_count), out_shape=jax.ShapeD...  17.4 us
    unnamed x1, local copies, waits for them, and re-layouts  1.57 us

profile of v4, /device:TPU:9, one launch (start us, length us, event | category | flops | bytes accessed | tf_op | source)
XLA Modules:
  0.0 18.9 jit_solution(12884062658637633280)
XLA Ops:
  0.0 17.4 %shard_map.55 = bf16[256,256]{1,0:T(8,128)(2,1)} custom-call(s32[1,256]{1,0:T(1,128)} %bitcast.1, bf16[3,4,2048]{2,1,0:T(4,128)(2,1)} %nuc_hbm.1, f32[3,7,2048]{2,1,0:T(8,128)} %short_hbm.1, f32[128,128]{1,0:T(8,128)} %mr_hbm.1, bf16[5,2048,256]{2,1,0:T(8,128)(2,1)} %head_hbm.1), custom_call_target="tpu_custom_call" | custom-call | tf_op jit(solution)/shard_map/pallas_call | solution.py:312
  17.4 1.6 %copy.7 = bf16[256,256]{1,0:T(8,128)(2,1)} copy(bf16[256,256]{1,0:T(8,128)(2,1)} %shard_map.55) | data formatting | bytes 262144

commit v5 on v4

--- a/solution.py
+++ b/solution.py
@@ -210,6 +210,18 @@
             for h in range(2):
                 track[h, s * half : (s + 1) * half, at] = turned[h * half : (h + 1) * half]
 
+    def add_head(part, d, at):
+        term = dot(track[part, :, at], head[d, at, :])
+        begin = pad + rim - d + part * half
+        total[begin : begin + half, :] += term[:half]
+        begin = pad + d - rim + part * half
+        total[begin : begin + half, :] += term[half:]
+
+    total[...] = jnp.zeros_like(total)
+    loads[4].wait()
+    first = slice(0, channels // 2)
+    second = slice(channels // 2, channels)
+    jobs = [(part, d) for d in range(head_taps) for part in range(2)]
     pending = []
     cells = gate(0)
     for p in range(part_count):
@@ -224,10 +236,14 @@
         if len(pending) == 3:
             turn(p - 2, pending[:2])
             pending = pending[2:]
+        if p > part_count // 2 + 1:
+            for part, d in jobs[:2]:
+                add_head(part, d, first)
+            jobs = jobs[2:]
     turn(part_count - len(pending), pending)
-
-    loads[4].wait()
-    total[...] = jnp.zeros_like(total)
+    for part, d in jobs:
+        add_head(part, d, first)
+
     cut = pad + half - 8
 
     def sum_copy(part):
@@ -255,11 +271,7 @@
 
     for part in range(2):
         for d in range(head_taps):
-            term = dot(track[part], head[d])
-            begin = pad + rim - d + part * half
-            total[begin : begin + half, :] += term[:half]
-            begin = pad + d - rim + part * half
-            total[begin : begin + half, :] += term[half:]
+            add_head(part, d, second)
         sum_copy(part).start()
 
         @pl.when(has_left if part == 0 else has_right)

time: 19.1 us -> 19.1 us (level)
  the two profiles are of different devices: /device:TPU:9 before, /device:TPU:0 now
where the time goes in v5:
time: 19.1 us; the launch traced here: 19 us
  Pallas kernels  17.4 us (91%)
  local copies, waits for them, and re-layouts  1.57 us (8%)
    pallas_call x1, Pallas kernels, shards(): pl.pallas_call(functools.partial(kernel, seq_count), out_shape=jax.ShapeD...  17.4 us
    unnamed x1, local copies, waits for them, and re-layouts  1.57 us

profile of v5, /device:TPU:0, one launch (start us, length us, event | category | flops | bytes accessed | tf_op | source)
XLA Modules:
  0.0 19.0 jit_solution(209798569822484826)
XLA Ops:
  0.0 17.4 %shard_map.55 = bf16[256,256]{1,0:T(8,128)(2,1)} custom-call(s32[1,256]{1,0:T(1,128)} %bitcast.1, bf16[3,4,2048]{2,1,0:T(4,128)(2,1)} %nuc_hbm.1, f32[3,7,2048]{2,1,0:T(8,128)} %short_hbm.1, f32[128,128]{1,0:T(8,128)} %mr_hbm.1, bf16[5,2048,256]{2,1,0:T(8,128)(2,1)} %head_hbm.1), custom_call_target="tpu_custom_call" | custom-call | tf_op jit(solution)/shard_map/pallas_call | solution.py:324
  17.4 1.6 %copy.7 = bf16[256,256]{1,0:T(8,128)(2,1)} copy(bf16[256,256]{1,0:T(8,128)(2,1)} %shard_map.55) | data formatting | bytes 262144
